TPU v7x, 512 devices: a whole 4x4x16 slice. The times are simulated.
512 devices in a mesh: dp: 32 (over y, x, core), sp: 16 (over z).
Axes of the slice: x: 4, y: 4, z: 16, core: 2. Of those that a mesh axis runs over, the one named last changes fastest.
Arguments:
- queries: bfloat16 [32768, 4096], P(('dp', 'sp'))
- keys: bfloat16 [32768, 1024], P(('dp', 'sp'))
- values: bfloat16 [32768, 1024], P(('dp', 'sp')), may hold values from -6 to 6
- positions: int32 [32768], P(('dp', 'sp')), may hold values from 0 to 1023, as said below
- piece_lengths: int32 [32, 16, 1], P('dp', 'sp'), may hold values from 1 to 64, as said below
- dest_group: int32 [32, 1], P('dp'), may hold values from 0 to 31, as said below
- dest_offset: int32 [32, 16, 1], P('dp', 'sp'), may hold values from 0 to 0, as said below
Outputs:
- packed_out: bfloat16 [32768, 4096], P(('dp', 'sp'))
Inputs may be any that keep to these rules, and one draw needn't show every extreme that they name: `piece_lengths`: the pieces of one sequence over the 16 devices of its instance sum to its length, which is 512 or more; the rows of a piece are the slot's first rows. dest_group[i, s] is i XOR m_s, where the numbers m_s depend on the slot s alone and differ from slot to slot; so every packed group is named by exactly one entry. `dest_offset`: on one device, the pieces arriving at one group lie back to back from row 0 in order of source instance and end at or before 64; in every draw some group is filled to exactly 64 rows on every device. The live rows of one sequence, over all its devices, hold the positions 0 to its length - 1, each once; rows that are not live hold 0.
All inputs are finite; a program needn't handle non-finite values.
Results may differ from a plain program's by a relative error of at most 0.0061.
Values may be sent and summed in bfloat16 or wider, within the bound.
A program may use at most 64 MiB of HBM per device.

v0:
```python
import functools

import jax
import jax.numpy as jnp
import numpy as np
from jax import lax
from jax.experimental import pallas as pl
from jax.experimental.pallas import tpu as pltpu
from jax.sharding import PartitionSpec as P

QH = 32
KVH = 8
D = 128
ROWS = 64
REP = QH // KVH
QROWS = REP * ROWS
THETA = 1000000.0
NEG = -1.0e30
FAR = 1 << 30
DIRECT = 4
SCALE = float(D ** -0.5 * np.log2(np.e))
MESH = pl.DeviceIdType.MESH


def frequencies():
    half = THETA ** (-(np.arange(D // 2, dtype=np.float64) * 2.0 / D))
    return np.concatenate([half, half])[None, :].astype(np.float32)


def kernel(n, mask, len_ref, q_ref, k_ref, v_ref, pos_ref, freq_ref, out_ref,
           kraw, vraw, qraw, praw, fraw, src, kpsrc, qsrc, kv, kp, rq, cap, o1, m1, l1,
           load, ksend, krecv, own_send, own_recv, psend, precv, pown_send, pown_recv, qsend, qrecv):
    z = lax.axis_index("sp")
    dp = lax.axis_index("dp")
    far = dp
    for bit in range(5):
        if mask >> bit & 1:
            far = far + (1 << bit) * (1 - 2 * lax.rem(lax.div(dp, 1 << bit), 2))
    right, left = lax.rem(z + 1, n), lax.rem(z + n - 1, n)
    half = n // 2
    OWN = half - 2
    FIRST = 3 * n // 4

    loads = [
        pltpu.make_async_copy(pos_ref, praw, load.at[0]),
        pltpu.make_async_copy(freq_ref, fraw, load.at[1]),
        pltpu.make_async_copy(k_ref, kraw, load.at[2]),
        pltpu.make_async_copy(v_ref, vraw, load.at[3]),
        pltpu.make_async_copy(q_ref, qraw, load.at[4]),
    ]
    for c in loads:
        c.start()
    peers = [(dp, left), (dp, right)]
    if mask:
        peers += [(far, z), (far, left), (far, right)]
    barrier = pltpu.get_barrier_semaphore()
    for peer in peers:
        pl.semaphore_signal(barrier, inc=1, device_id=peer, device_id_type=MESH)

    length = len_ref[0]
    rows = lax.broadcasted_iota(jnp.int32, (ROWS, D), 0)
    lanes = lax.broadcasted_iota(jnp.int32, (ROWS, D), 1)
    diag = rows == lax.rem(lanes, ROWS)
    live = rows < length
    loads[0].wait()
    loads[1].wait()
    pos_wide = jnp.broadcast_to(jnp.concatenate([praw[...], praw[...]], axis=1), (ROWS, D))
    pos_col = jnp.sum(jnp.where(rows == lanes, pos_wide, 0), axis=1, keepdims=True)
    angle = pos_col.astype(jnp.float32) * fraw[...]
    cosine = jnp.cos(angle)
    sine = jnp.sin(angle)
    sine = jnp.where(lanes < D // 2, -sine, sine)

    def rotate(x):
        x = x.astype(jnp.float32)
        return x * cosine + pltpu.roll(x, D // 2, 1) * sine

    key_pos = jnp.min(jnp.where(diag & live, pos_col, FAR), axis=0, keepdims=True)
    key_pos = jnp.broadcast_to(key_pos, (8, D))
    if mask:
        kpsrc[...] = key_pos
    else:
        kp[OWN] = key_pos
    loads[2].wait()
    loads[3].wait()
    for h in range(KVH):
        cols = pl.ds(h * D, D)
        rk = jnp.where(live, rotate(kraw[:, cols]), 0.0).astype(jnp.bfloat16)
        if mask:
            src[h, 0] = rk
            src[h, 1] = vraw[:, cols]
        else:
            kv[h, OWN, 0] = rk
            kv[h, OWN, 1] = vraw[:, cols]

    def slot(s):
        return lax.rem(s + OWN, n)

    def reach(h):
        return (half, n - 1 - half) if h % 2 == 0 else (n - 1 - half, half)

    def remote(a, b, s, r, device):
        return pltpu.make_async_remote_copy(
            src_ref=a, dst_ref=b, send_sem=s, recv_sem=r, device_id=device, device_id_type=MESH)

    def at(d, to_right):
        return slot(d) if to_right else slot(n - d)

    def copy(h, d, to_right):
        a, b = at(d, to_right), at(d + 1, to_right)
        return remote(kv.at[h, a], kv.at[h, b], ksend.at[0 if to_right else 1, h, d],
                      krecv.at[h, b], (dp, right if to_right else left))

    def pcopy(d, to_right):
        a, b = at(d, to_right), at(d + 1, to_right)
        return remote(kp.at[a], kp.at[b], psend.at[0 if to_right else 1, d],
                      precv.at[b], (dp, right if to_right else left))

    def own(h):
        return remote(src.at[h], kv.at[h, OWN], own_send.at[h, 0], own_recv.at[h], (far, z))

    def direct(h, to_right):
        b = at(1, to_right)
        return remote(src.at[h], kv.at[h, b], own_send.at[h, 1 if to_right else 2],
                      krecv.at[h, b], (far, right if to_right else left))

    def pown():
        return remote(kpsrc, kp.at[OWN], pown_send.at[0], pown_recv.at[0], (far, z))

    def pdirect(to_right):
        b = at(1, to_right)
        return remote(kpsrc, kp.at[b], pown_send.at[1 if to_right else 2],
                      precv.at[b], (far, right if to_right else left))

    def qcopy(h):
        return remote(qsrc.at[h], rq.at[h], qsend.at[h], qrecv.at[h], (far, z))

    pl.semaphore_wait(barrier, len(peers))

    BOTH = (True, False)
    straight = DIRECT if mask else 0
    if mask:
        for h in range(straight):
            direct(h, True).start()
            direct(h, False).start()
            if h == 0:
                for h2 in range(straight, KVH):
                    own(h2).start()
        for r in BOTH:
            pdirect(r).start()
        pown().start()
        for h in range(straight):
            own(h).start()
    else:
        for r in BOTH:
            pcopy(0, r).start()
    for h in range(straight, KVH):
        if mask:
            own(h).wait_recv()
        for r in BOTH:
            copy(h, 0, r).start()

    def step(d):
        for r in BOTH:
            pcopy(d - 1, r).wait_recv()
            pcopy(d, r).start()
        for h in range(KVH):
            for r in BOTH:
                copy(h, d - 1, r).wait_recv()
                copy(h, d, r).start()

    loads[4].wait()

    def early(d, _):
        step(d)
        for e in range(2):
            h = (d - 1) * 2 + e
            for g in range(REP):
                cols = pl.ds(pl.multiple_of((h * REP + g) * D, D), D)
                x = rotate(qraw[:, cols]).astype(jnp.bfloat16)
                if mask:
                    qsrc[h, g * ROWS:(g + 1) * ROWS] = x
                else:
                    rq[h, g * ROWS:(g + 1) * ROWS] = x
            if mask:
                qcopy(h).start()
        return 0

    lax.fori_loop(1, 5, early, 0)

    def middle(d, _):
        step(d)
        return 0

    lax.fori_loop(5, half - 2, middle, 0)

    if mask:
        pown().wait_recv()
        for h in range(straight):
            own(h).wait_recv()
    q_row = kp[OWN][0:1]
    q_col = jnp.min(jnp.where(rows == lanes, jnp.broadcast_to(q_row, (ROWS, D)), FAR),
                    axis=1, keepdims=True)
    q_live = q_col < FAR

    def build_cap(first, last):
        for t in range(first // 2, last // 2):
            pair = jnp.where(lanes[0:1] < ROWS, kp[2 * t, 0:1], kp[2 * t + 1, 0:1])
            cap[:, t * D:(t + 1) * D] = jnp.where(
                jnp.broadcast_to(pair, (ROWS, D)) <= q_col, jnp.float32(jnp.inf), NEG)

    def scores(h, first, last):
        keys = kv[h, first:last, 0].reshape((last - first) * ROWS, D)
        s = lax.dot_general(rq[h], keys, (((1,), (1,)), ((), ())),
                            preferred_element_type=jnp.float32)
        c = cap[:, first * ROWS:last * ROWS]
        s = jnp.minimum(s, jnp.concatenate([c] * REP, axis=0))
        return s, jnp.max(s, axis=1, keepdims=True)

    def weigh(h, s, m, first, last):
        vals = kv[h, first:last, 1].reshape((last - first) * ROWS, D)
        w = jnp.exp2(s * SCALE - m * SCALE)
        return jnp.sum(w, axis=1, keepdims=True), jnp.dot(
            w.astype(jnp.bfloat16), vals, preferred_element_type=jnp.float32)

    def part_one(h):
        if mask:
            qcopy(h).wait_recv()
        s, m = scores(h, 0, FIRST)
        total, o = weigh(h, s, m, 0, FIRST)
        o1[h] = o
        m1[h] = jnp.broadcast_to(m, (QROWS, D))
        l1[h] = jnp.broadcast_to(total, (QROWS, D))

    def part_two(h):
        s, m = scores(h, FIRST, n)
        m = jnp.maximum(m, m1[h][:, 0:1])
        total, o = weigh(h, s, m, FIRST, n)
        a = jnp.exp2((m1[h] - m) * SCALE)
        o = (o1[h] * a + o) / (l1[h] * a + total)
        parts = [jnp.where(q_live, o[g * ROWS:(g + 1) * ROWS], 0.0) for g in range(REP)]
        out_ref[:, pl.ds(pl.multiple_of(h * REP * D, D), REP * D)] = jnp.concatenate(
            parts, axis=1).astype(jnp.bfloat16)

    d = half - 2
    for r in BOTH:
        pcopy(d - 1, r).wait_recv()
        pcopy(d, r).start()
    build_cap(0, FIRST)

    def six(j, _):
        for e in range(2):
            h = 2 * j + e
            for r in BOTH:
                copy(h, d - 1, r).wait_recv()
                copy(h, d, r).start()
        part_one(j)
        return 0

    lax.fori_loop(0, KVH // 2, six, 0)
    for r in BOTH:
        pcopy(d, r).wait_recv()
    pcopy(d + 1, True).start()

    def seven(j, _):
        for e in range(2):
            h = 2 * j + e
            for r in BOTH:
                copy(h, d, r).wait_recv()
            copy(h, d + 1, e == 0).start()
        part_one(KVH // 2 + j)
        return 0

    lax.fori_loop(0, KVH // 2, seven, 0)
    pcopy(d + 1, True).wait_recv()
    build_cap(FIRST, n)

    def eight(j, _):
        for e in range(2):
            h = 2 * j + e
            copy(h, d + 1, e == 0).wait_recv()
            part_two(h)
        return 0

    lax.fori_loop(0, KVH // 2, eight, 0)

    if mask:
        for r in BOTH:
            pdirect(r).wait_send()
        pown().wait_send()
        for h in range(KVH):
            own(h).wait_send()
            qcopy(h).wait_send()
        for h in range(straight):
            for r in BOTH:
                direct(h, r).wait_send()
    else:
        for r in BOTH:
            pcopy(0, r).wait_send()
    for h in range(straight, KVH):
        for r in BOTH:
            copy(h, 0, r).wait_send()

    def drain(d, _):
        for r in BOTH:
            pcopy(d, r).wait_send()
            for h in range(KVH):
                copy(h, d, r).wait_send()
        return 0

    lax.fori_loop(1, half - 1, drain, 0)
    pcopy(half - 1, True).wait_send()
    for h in range(KVH):
        copy(h, half - 1, h % 2 == 0).wait_send()


def attend(mask, n, *operands):
    vm = pl.BlockSpec(memory_space=pltpu.VMEM)
    sm = pl.BlockSpec(memory_space=pltpu.SMEM)
    hbm = pl.BlockSpec(memory_space=pl.ANY)
    dma = pltpu.SemaphoreType.DMA
    b16, f32, i32 = jnp.bfloat16, jnp.float32, jnp.int32
    half = n // 2
    return pl.pallas_call(
        functools.partial(kernel, n, mask),
        out_shape=jax.ShapeDtypeStruct((ROWS, QH * D), b16),
        in_specs=[sm, hbm, hbm, hbm, hbm, hbm],
        out_specs=vm,
        scratch_shapes=[
            pltpu.VMEM((ROWS, KVH * D), b16),
            pltpu.VMEM((ROWS, KVH * D), b16),
            pltpu.VMEM((ROWS, QH * D), b16),
            pltpu.VMEM((1, ROWS), i32),
            pltpu.VMEM((1, D), f32),
            pltpu.VMEM((KVH, 2, ROWS, D), b16),
            pltpu.VMEM((8, D), i32),
            pltpu.VMEM((KVH, QROWS, D), b16),
            pltpu.VMEM((KVH, n, 2, ROWS, D), b16),
            pltpu.VMEM((n, 8, D), i32),
            pltpu.VMEM((KVH, QROWS, D), b16),
            pltpu.VMEM((ROWS, n * ROWS), f32),
            pltpu.VMEM((KVH, QROWS, D), f32),
            pltpu.VMEM((KVH, QROWS, D), f32),
            pltpu.VMEM((KVH, QROWS, D), f32),
            dma((5,)),
            dma((2, KVH, half)), dma((KVH, n)),
            dma((KVH, 3)), dma((KVH,)),
            dma((2, half)), dma((n,)),
            dma((3,)), dma((1,)),
            dma((KVH,)), dma((KVH,)),
        ],
        compiler_params=pltpu.CompilerParams(
            collective_id=mask, has_side_effects=True, vmem_limit_bytes=56 * 1024 * 1024),
        name="gather_attend",
    )(*operands)


def on_device(queries, keys, values, positions, piece_lengths, dest_group, dest_offset):
    n = lax.axis_size("sp")
    groups = lax.axis_size("dp")
    mask = dest_group[0, 0] ^ lax.axis_index("dp")
    out = attend(0, n, piece_lengths.reshape(1), queries, keys, values,
                 positions.reshape(1, ROWS), jnp.asarray(frequencies()))
    return lax.switch(mask, [
        functools.partial(lambda m, x: lax.ppermute(x, "dp", [(i, i ^ m) for i in range(groups)]), m)
        for m in range(groups)
    ], out)


def solution(mesh):
    in_specs = (
        P(("dp", "sp"), None), P(("dp", "sp"), None), P(("dp", "sp"), None), P(("dp", "sp")),
        P("dp", "sp", None), P("dp", None), P("dp", "sp", None),
    )
    return jax.shard_map(on_device, mesh=mesh, in_specs=in_specs,
                         out_specs=P(("dp", "sp"), None), check_vma=False)
```

profile of v0, /device:TPU:16, one launch (start us, length us, event | category | flops | bytes accessed | tf_op | source)
XLA Modules:
  0.0 81.7 jit_solution(6930107914831959990)
XLA Ops:
  1.3 61.2 %gather_attend.1 = bf16[64,4096]{1,0:T(8,128)(2,1)S(1)} custom-call(s32[1]{0:T(128)} %bitcast.3.len_ref, bf16[64,4096]{1,0:T(8,128)(2,1)} %q_ref.1, bf16[64,1024]{1,0:T(8,128)(2,1)} %k_ref.1, bf16[64,1024]{1,0:T(8,128)(2,1)} %v_ref.1, s32[1,64]{1,0:T(1,128)} %bitcast.5, f32[1,128]{1,0:T(1,128)} %constant.12.clone.freq_ref), custom_call_target="tpu_custom_call" | custom-call | tf_op jit(solution)/shard_map/gather_attend/pallas_call | solution.py:324
  62.5 17.4 %conditional.1 = (bf16[64,4096]{1,0:T(8,128)(2,1)}) conditional(s32[]{:T(128)} %clamp.3, bf16[64,4096]{1,0:T(8,128)(2,1)S(1)} %gather_attend.1, bf16[64,4096]{1,0:T(8,128)(2,1)S(1)} %gather_attend.1, bf16[64,4096]{1,0:T(8,128)(2,1)S(1)} %gather_attend.1, bf16[64,4096]{1,0:T(8,128)(2,1)S(1)} %gather_attend.1, ...), branch_computations={%region_0.0_spmd, %region_1.0_spmd, %region_2.0_spmd, %region_3.0_... | conditional | bytes 2097200 | solution.py:364
  62.5 2.7 %collective-permute-start.7 = (bf16[64,4096]{1,0:T(8,128)(2,1)S(1)}, bf16[64,4096]{1,0:T(8,128)(2,1)}, u32[]{:S(2)}, u32[]{:S(2)}) collective-permute-start(bf16[64,4096]{1,0:T(8,128)(2,1)S(1)} %param.7), channel_id=1, source_target_pairs={{0,112},{16,96},{32,80},{48,64},{64,48},{80,32},{96,16},{112,0},{1... | collective-permute-start | bytes 1572872 | tf_op jit(solution)/shard_map/cond/branch_7_fun/ppermute | solution.py:365
  65.3 14.6 %collective-permute-done.7 = bf16[64,4096]{1,0:T(8,128)(2,1)} collective-permute-done((bf16[64,4096]{1,0:T(8,128)(2,1)S(1)}, bf16[64,4096]{1,0:T(8,128)(2,1)}, u32[]{:S(2)}, u32[]{:S(2)}) %collective-permute-start.7) | collective-permute-done | bytes 524320 | tf_op jit(solution)/shard_map/cond/branch_7_fun/ppermute | solution.py:365
  79.9 1.9 %copy.75 = bf16[64,4096]{1,0:T(8,128)(2,1)} copy(bf16[64,4096]{1,0:T(8,128)(2,1)} %get-tuple-element.70) | data formatting | bytes 1048576
Async XLA Ops:
  62.5 17.3 %collective-permute-start.7 = (bf16[64,4096]{1,0:T(8,128)(2,1)S(1)}, bf16[64,4096]{1,0:T(8,128)(2,1)}, u32[]{:S(2)}, u32[]{:S(2)}) collective-permute-start(bf16[64,4096]{1,0:T(8,128)(2,1)S(1)} %param.7), channel_id=1, source_target_pairs={{0,112},{16,96},{32,80},{48,64},{64,48},{80,32},{96,16},{112,0},{1... | collective-permute-start | bytes 1572872 | tf_op jit(solution)/shard_map/cond/branch_7_fun/ppermute | solution.py:365
where the time goes:
time: 81 us; the launch traced here: 81.7 us
  Pallas kernels  61.2 us (76%)
  waiting for transfers between devices  14.6 us (18%)
  starting transfers between devices  2.73 us (3%)
  local copies, waits for them, and re-layouts  1.87 us (2%)
  between operations  1.31 us (2%)
    pallas_call x1, Pallas kernels, attend(): pl.pallas_call(functools.partial(kernel, n, mask), out_shape=jax.ShapeDty...  61.2 us
    ppermute x1, waiting for transfers between devices, on_device(): lax.ppermute(x, 'dp', [(i, i ^ m) for i in range(groups)])  14.6 us
    ppermute x1, starting transfers between devices, on_device(): lax.ppermute(x, 'dp', [(i, i ^ m) for i in range(groups)])  2.73 us
    unnamed x1, local copies, waits for them, and re-layouts  1.87 us
  transfers between devices with their start and end apart: 1, of which 1 were waited for; matrix products, arithmetic and copies ran while one was open for 0% of the time, Pallas kernels for 0%

commit v1 on v0

v1 whole, which is shorter than its diff:
```python
import functools

import jax
import jax.numpy as jnp
import numpy as np
from jax import lax
from jax.experimental import pallas as pl
from jax.experimental.pallas import tpu as pltpu
from jax.sharding import PartitionSpec as P

QH = 32
KVH = 8
D = 128
ROWS = 64
REP = QH // KVH
QROWS = REP * ROWS
THETA = 1000000.0
NEG = -1.0e30
FAR = 1 << 30
SCALE = float(D ** -0.5 * np.log2(np.e))
MESH = pl.DeviceIdType.MESH


def frequencies():
    half = THETA ** (-(np.arange(D // 2, dtype=np.float64) * 2.0 / D))
    return np.concatenate([half, half])[None, :].astype(np.float32)


def kernel(n, len_ref, q_ref, k_ref, v_ref, pos_ref, freq_ref, out_ref,
           lraw, kraw, vraw, qraw, praw, fraw, kv, kp, rq, cap, o1, m1, l1,
           load, ksend, krecv, vsend, vrecv, psend, precv):
    z = lax.axis_index("sp")
    dp = lax.axis_index("dp")
    right, left = lax.rem(z + 1, n), lax.rem(z + n - 1, n)
    half = n // 2
    OWN = half - 2
    FIRST = 3 * n // 4

    loads = [
        pltpu.make_async_copy(pos_ref, praw, load.at[0]),
        pltpu.make_async_copy(freq_ref, fraw, load.at[1]),
        pltpu.make_async_copy(k_ref, kraw, load.at[2]),
        pltpu.make_async_copy(v_ref, vraw, load.at[3]),
        pltpu.make_async_copy(q_ref, qraw, load.at[4]),
        pltpu.make_async_copy(len_ref, lraw, load.at[5]),
    ]
    for c in loads:
        c.start()
    peers = [(dp, left), (dp, right)]
    barrier = pltpu.get_barrier_semaphore()
    for peer in peers:
        pl.semaphore_signal(barrier, inc=1, device_id=peer, device_id_type=MESH)

    rows = lax.broadcasted_iota(jnp.int32, (ROWS, D), 0)
    lanes = lax.broadcasted_iota(jnp.int32, (ROWS, D), 1)
    diag = rows == lax.rem(lanes, ROWS)
    def slot(s):
        return lax.rem(s + OWN, n)

    def reach(h):
        return (half, n - 1 - half) if h % 2 == 0 else (n - 1 - half, half)

    def remote(a, b, s, r, device):
        return pltpu.make_async_remote_copy(
            src_ref=a, dst_ref=b, send_sem=s, recv_sem=r, device_id=device, device_id_type=MESH)

    def at(d, to_right):
        return slot(d) if to_right else slot(n - d)

    def copy(h, d, to_right):
        a, b = at(d, to_right), at(d + 1, to_right)
        return remote(kv.at[h, a], kv.at[h, b], ksend.at[0 if to_right else 1, h, d],
                      krecv.at[h, b], (dp, right if to_right else left))

    def pcopy(d, to_right):
        a, b = at(d, to_right), at(d + 1, to_right)
        return remote(kp.at[a], kp.at[b], psend.at[0 if to_right else 1, d],
                      precv.at[b], (dp, right if to_right else left))

    def vcopy(h, to_right):
        a, b = at(0, to_right), at(1, to_right)
        side = 0 if to_right else 1
        return remote(kv.at[h, a, 1], kv.at[h, b, 1], vsend.at[side, h], vrecv.at[side, h],
                      (dp, right if to_right else left))

    def kcopy(h, to_right):
        a, b = at(0, to_right), at(1, to_right)
        return remote(kv.at[h, a, 0], kv.at[h, b, 0], ksend.at[0 if to_right else 1, h, 0],
                      krecv.at[h, b], (dp, right if to_right else left))

    BOTH = (True, False)
    loads[3].wait()
    for h in range(KVH):
        kv[h, OWN, 1] = vraw[:, h * D:(h + 1) * D]
    pl.semaphore_wait(barrier, len(peers))
    for h in range(KVH):
        for r in BOTH:
            vcopy(h, r).start()

    for i in (5, 0, 1):
        loads[i].wait()
    live = rows < lraw[0, 0, 0]
    pos_wide = jnp.broadcast_to(jnp.concatenate([praw[...], praw[...]], axis=1), (ROWS, D))
    pos_col = jnp.sum(jnp.where(rows == lanes, pos_wide, 0), axis=1, keepdims=True)
    angle = pos_col.astype(jnp.float32) * fraw[...]
    cosine = jnp.cos(angle)
    sine = jnp.sin(angle)
    sine = jnp.where(lanes < D // 2, -sine, sine)

    def rotate(x):
        x = x.astype(jnp.float32)
        return x * cosine + pltpu.roll(x, D // 2, 1) * sine

    loads[2].wait()
    for h in range(KVH):
        rk = jnp.where(live, rotate(kraw[:, h * D:(h + 1) * D]), 0.0)
        kv[h, OWN, 0] = rk.astype(jnp.bfloat16)
        for r in BOTH:
            kcopy(h, r).start()
    key_pos = jnp.min(jnp.where(diag & live, pos_col, FAR), axis=0, keepdims=True)
    kp[OWN] = jnp.broadcast_to(key_pos, (8, D))
    for r in BOTH:
        pcopy(0, r).start()

    def step(d):
        for r in BOTH:
            pcopy(d - 1, r).wait_recv()
            pcopy(d, r).start()
        for h in range(KVH):
            for r in BOTH:
                copy(h, d - 1, r).wait_recv()
                copy(h, d, r).start()

    for h in range(KVH):
        for r in BOTH:
            vcopy(h, r).wait_recv()
            kcopy(h, r).wait_recv()
            copy(h, 1, r).start()
    for r in BOTH:
        pcopy(0, r).wait_recv()
        pcopy(1, r).start()
    loads[4].wait()

    def rotate_q(h):
        for g in range(REP):
            cols = pl.ds(pl.multiple_of((h * REP + g) * D, D), D)
            rq[h, g * ROWS:(g + 1) * ROWS] = rotate(qraw[:, cols]).astype(jnp.bfloat16)

    def early(d, _):
        for e in range(2):
            rotate_q((d - 2) * 2 + e)
        step(d)
        return 0

    lax.fori_loop(2, half - 2, early, 0)

    q_row = kp[OWN][0:1]
    q_col = jnp.min(jnp.where(rows == lanes, jnp.broadcast_to(q_row, (ROWS, D)), FAR),
                    axis=1, keepdims=True)
    q_live = q_col < FAR

    def build_cap(first, last):
        for t in range(first // 2, last // 2):
            pair = jnp.where(lanes[0:1] < ROWS, kp[2 * t, 0:1], kp[2 * t + 1, 0:1])
            cap[:, t * D:(t + 1) * D] = jnp.where(
                jnp.broadcast_to(pair, (ROWS, D)) <= q_col, jnp.float32(jnp.inf), NEG)

    def scores(h, first, last):
        keys = kv[h, first:last, 0].reshape((last - first) * ROWS, D)
        s = lax.dot_general(rq[h], keys, (((1,), (1,)), ((), ())),
                            preferred_element_type=jnp.float32)
        c = cap[:, first * ROWS:last * ROWS]
        s = jnp.minimum(s, jnp.concatenate([c] * REP, axis=0))
        return s, jnp.max(s, axis=1, keepdims=True)

    def weigh(h, s, m, first, last):
        vals = kv[h, first:last, 1].reshape((last - first) * ROWS, D)
        w = jnp.exp2(s * SCALE - m * SCALE)
        return jnp.sum(w, axis=1, keepdims=True), jnp.dot(
            w.astype(jnp.bfloat16), vals, preferred_element_type=jnp.float32)

    def part_one(h):
        s, m = scores(h, 0, FIRST)
        total, o = weigh(h, s, m, 0, FIRST)
        o1[h] = o
        m1[h] = jnp.broadcast_to(m, (QROWS, D))
        l1[h] = jnp.broadcast_to(total, (QROWS, D))

    def part_two(h):
        s, m = scores(h, FIRST, n)
        m = jnp.maximum(m, m1[h][:, 0:1])
        total, o = weigh(h, s, m, FIRST, n)
        a = jnp.exp2((m1[h] - m) * SCALE)
        o = (o1[h] * a + o) / (l1[h] * a + total)
        parts = [jnp.where(q_live, o[g * ROWS:(g + 1) * ROWS], 0.0) for g in range(REP)]
        out_ref[:, pl.ds(pl.multiple_of(h * REP * D, D), REP * D)] = jnp.concatenate(
            parts, axis=1).astype(jnp.bfloat16)

    d = half - 2
    for r in BOTH:
        pcopy(d - 1, r).wait_recv()
        pcopy(d, r).start()
    build_cap(0, FIRST)

    def six(j, _):
        for e in range(2):
            h = 2 * j + e
            for r in BOTH:
                copy(h, d - 1, r).wait_recv()
                copy(h, d, r).start()
        part_one(j)
        return 0

    lax.fori_loop(0, KVH // 2, six, 0)
    for r in BOTH:
        pcopy(d, r).wait_recv()
    pcopy(d + 1, True).start()

    def seven(j, _):
        for e in range(2):
            h = 2 * j + e
            for r in BOTH:
                copy(h, d, r).wait_recv()
            copy(h, d + 1, e == 0).start()
        part_one(KVH // 2 + j)
        return 0

    lax.fori_loop(0, KVH // 2, seven, 0)
    pcopy(d + 1, True).wait_recv()
    build_cap(FIRST, n)

    def eight(j, _):
        for e in range(2):
            h = 2 * j + e
            copy(h, d + 1, e == 0).wait_recv()
            part_two(h)
        return 0

    lax.fori_loop(0, KVH // 2, eight, 0)

    for r in BOTH:
        pcopy(0, r).wait_send()
        for h in range(KVH):
            vcopy(h, r).wait_send()
            kcopy(h, r).wait_send()

    def drain(d, _):
        for r in BOTH:
            pcopy(d, r).wait_send()
            for h in range(KVH):
                copy(h, d, r).wait_send()
        return 0

    lax.fori_loop(1, half - 1, drain, 0)
    pcopy(half - 1, True).wait_send()
    for h in range(KVH):
        copy(h, half - 1, h % 2 == 0).wait_send()


def attend(n, *operands):
    vm = pl.BlockSpec(memory_space=pltpu.VMEM)
    hbm = pl.BlockSpec(memory_space=pl.ANY)
    dma = pltpu.SemaphoreType.DMA
    b16, f32, i32 = jnp.bfloat16, jnp.float32, jnp.int32
    half = n // 2
    return pl.pallas_call(
        functools.partial(kernel, n),
        out_shape=jax.ShapeDtypeStruct((ROWS, QH * D), b16),
        in_specs=[hbm, hbm, hbm, hbm, hbm, hbm],
        out_specs=vm,
        scratch_shapes=[
            pltpu.SMEM((1, 1, 1), i32),
            pltpu.VMEM((ROWS, KVH * D), b16),
            pltpu.VMEM((ROWS, KVH * D), b16),
            pltpu.VMEM((ROWS, QH * D), b16),
            pltpu.VMEM((1, ROWS), i32),
            pltpu.VMEM((1, D), f32),
            pltpu.VMEM((KVH, n, 2, ROWS, D), b16),
            pltpu.VMEM((n, 8, D), i32),
            pltpu.VMEM((KVH, QROWS, D), b16),
            pltpu.VMEM((ROWS, n * ROWS), f32),
            pltpu.VMEM((KVH, QROWS, D), f32),
            pltpu.VMEM((KVH, QROWS, D), f32),
            pltpu.VMEM((KVH, QROWS, D), f32),
            dma((6,)),
            dma((2, KVH, half)), dma((KVH, n)),
            dma((2, KVH)), dma((2, KVH)),
            dma((2, half)), dma((n,)),
        ],
        compiler_params=pltpu.CompilerParams(
            collective_id=0, has_side_effects=True, vmem_limit_bytes=56 * 1024 * 1024),
        name="gather_attend",
    )(*operands)


def place_kernel(x_ref, out_ref, done):
    copies = []
    for p in range(8):
        part = (pl.ds(p // 2 * 16, 16), pl.ds(p % 2 * (QH * D // 2), QH * D // 2))
        copies.append(pltpu.make_async_copy(x_ref.at[part], out_ref.at[part], done.at[p]))
    for c in copies:
        c.start()
    for c in copies:
        c.wait()


def place(x):
    hbm = pl.BlockSpec(memory_space=pl.ANY)
    return pl.pallas_call(
        place_kernel, out_shape=jax.ShapeDtypeStruct(x.shape, x.dtype), in_specs=[hbm],
        out_specs=hbm, scratch_shapes=[pltpu.SemaphoreType.DMA((8,))], name="place",
    )(x)


def on_device(queries, keys, values, positions, piece_lengths, dest_group, dest_offset):
    n = lax.axis_size("sp")
    groups = lax.axis_size("dp")
    mask = dest_group[0, 0] ^ lax.axis_index("dp")
    out = attend(n, piece_lengths, queries, keys, values,
                 positions.reshape(1, ROWS), jnp.asarray(frequencies()))
    return place(lax.switch(mask, [
        functools.partial(lambda m, x: lax.ppermute(x, "dp", [(i, i ^ m) for i in range(groups)]), m)
        for m in range(groups)
    ], out))


def solution(mesh):
    in_specs = (
        P(("dp", "sp"), None), P(("dp", "sp"), None), P(("dp", "sp"), None), P(("dp", "sp")),
        P("dp", "sp", None), P("dp", None), P("dp", "sp", None),
    )
    return jax.shard_map(on_device, mesh=mesh, in_specs=in_specs,
                         out_specs=P(("dp", "sp"), None), check_vma=False)
```

time: 81 us -> 94.6 us (1.17); the launches traced: 81.7 us -> 94.4 us
  Pallas kernels: 61.2 us -> 80.2 us
  waiting for transfers between devices: 14.6 us -> 9.45 us
  local copies, waits for them, and re-layouts: 1.87 us -> 0 us
    pallas_call x1 -> x2, Pallas kernels: 61.2 us -> 80.2 us  [the longest x1 63.1 us: attend(): pl.pallas_call(functools.partial(kernel, n), out_shape=jax.ShapeDtypeStru...]
    ppermute x1, waiting for transfers between devices: 14.6 us -> 9.45 us  [on_device(): lax.ppermute(x, 'dp', [(i, i ^ m) for i in range(groups)])]
    unnamed x1 -> x0, local copies, waits for them, and re-layouts: 1.87 us -> none
where the time goes in v1:
time: 94.6 us; the launch traced here: 94.4 us
  Pallas kernels  80.2 us (85%)
  waiting for transfers between devices  9.45 us (10%)
  starting transfers between devices  3.4 us (4%)
  between operations  1.31 us (1%)
    pallas_call x1, Pallas kernels, attend(): pl.pallas_call(functools.partial(kernel, n), out_shape=jax.ShapeDtypeStru...  63.1 us
    pallas_call x1, Pallas kernels, place(): pl.pallas_call(place_kernel, out_shape=jax.ShapeDtypeStruct(x.shape, x.dt...  17.1 us
    ppermute x1, waiting for transfers between devices, on_device(): lax.ppermute(x, 'dp', [(i, i ^ m) for i in range(groups)])  9.45 us
    ppermute x1, starting transfers between devices, on_device(): lax.ppermute(x, 'dp', [(i, i ^ m) for i in range(groups)])  3.4 us
  transfers between devices with their start and end apart: 1, of which 1 were waited for; matrix products, arithmetic and copies ran while one was open for 0% of the time, Pallas kernels for 0%

profile of v1, /device:TPU:16, one launch (start us, length us, event | category | flops | bytes accessed | tf_op | source)
XLA Modules:
  0.0 94.4 jit_solution(15830279112899191172)
XLA Ops:
  1.3 63.1 %gather_attend.1 = bf16[64,4096]{1,0:T(8,128)(2,1)S(1)} custom-call(s32[1,1,1]{2,1,0:T(1,128)S(6)} %copy.40.len_ref, bf16[64,4096]{1,0:T(8,128)(2,1)} %q_ref.1, bf16[64,1024]{1,0:T(8,128)(2,1)} %k_ref.1, bf16[64,1024]{1,0:T(8,128)(2,1)} %v_ref.1, s32[1,64]{1,0:T(1,128)} %bitcast.3, f32[1,128]{1,0:T(1,128)} %constant.12.clone.freq_ref), custom_call_target="tpu_custom_call" | custom-call | tf_op jit(solution)/shard_map/gather_attend/pallas_call | solution.py:266
  64.4 12.9 %conditional.1 = (bf16[64,4096]{1,0:T(8,128)(2,1)}) conditional(s32[]{:T(128)} %clamp.3, bf16[64,4096]{1,0:T(8,128)(2,1)S(1)} %gather_attend.1, bf16[64,4096]{1,0:T(8,128)(2,1)S(1)} %gather_attend.1, bf16[64,4096]{1,0:T(8,128)(2,1)S(1)} %gather_attend.1, bf16[64,4096]{1,0:T(8,128)(2,1)S(1)} %gather_attend.1, ...), branch_computations={%region_0.0_spmd, %region_1.0_spmd, %region_2.0_spmd, %region_3.0_... | conditional | bytes 2097200 | solution.py:321
  64.5 3.4 %collective-permute-start.2 = (bf16[64,4096]{1,0:T(8,128)(2,1)S(1)}, bf16[64,4096]{1,0:T(8,128)(2,1)}, u32[]{:S(2)}, u32[]{:S(2)}) collective-permute-start(bf16[64,4096]{1,0:T(8,128)(2,1)S(1)} %param.2), channel_id=1, source_target_pairs={{0,32},{16,48},{32,0},{48,16},{64,96},{80,112},{96,64},{112,80},{1... | collective-permute-start | bytes 1572872 | tf_op jit(solution)/shard_map/cond/branch_2_fun/ppermute | solution.py:322
  67.9 9.5 %collective-permute-done.2 = bf16[64,4096]{1,0:T(8,128)(2,1)} collective-permute-done((bf16[64,4096]{1,0:T(8,128)(2,1)S(1)}, bf16[64,4096]{1,0:T(8,128)(2,1)}, u32[]{:S(2)}, u32[]{:S(2)}) %collective-permute-start.2) | collective-permute-done | bytes 524320 | tf_op jit(solution)/shard_map/cond/branch_2_fun/ppermute | solution.py:322
  77.3 17.1 %place.1 = bf16[64,4096]{1,0:T(8,128)(2,1)} custom-call(bf16[64,4096]{1,0:T(8,128)(2,1)} %get-tuple-element.70.x_ref), custom_call_target="tpu_custom_call" | custom-call | tf_op jit(solution)/shard_map/place/pallas_call | solution.py:309
Async XLA Ops:
  64.5 12.9 %collective-permute-start.2 = (bf16[64,4096]{1,0:T(8,128)(2,1)S(1)}, bf16[64,4096]{1,0:T(8,128)(2,1)}, u32[]{:S(2)}, u32[]{:S(2)}) collective-permute-start(bf16[64,4096]{1,0:T(8,128)(2,1)S(1)} %param.2), channel_id=1, source_target_pairs={{0,32},{16,48},{32,0},{48,16},{64,96},{80,112},{96,64},{112,80},{1... | collective-permute-start | bytes 1572872 | tf_op jit(solution)/shard_map/cond/branch_2_fun/ppermute | solution.py:322
